TPU v7x, 256 devices: a whole 4x4x8 slice. The times are simulated.
256 devices in a mesh: cores: 2 (over core), row: 16 (over y, x), vec: 8 (over z).
Axes of the slice: x: 4, y: 4, z: 8, core: 2. Of those that a mesh axis runs over, the one named last changes fastest.
Arguments:
- train_cores: float32 [8, 512, 256, 256], P('vec', 'cores', 'row'), may hold values from -0.01953125 to 0.01953125
- sketch: float32 [512, 128], P('cores'), may hold values from -6 to 6
- exit_sketch: float32 [256, 128], replicated, may hold values from -6 to 6
Outputs:
- rounded: float32 [8, 256, 256, 128], P('vec', 'cores', 'row')
- interface_bases: float32 [8, 512, 128], P('vec', 'cores')
- margins: float32 [8, 256, 1024], P('vec', 'cores')
All inputs are finite; a program needn't handle non-finite values.
Results may differ from a plain program's by a relative error of at most 0.0003.
Values sent between devices are 32-bit elements; how exact they have to be, the bound alone decides.
A program may use at most 128 MiB of HBM per device.

v0:
```python
import math
import jax
import jax.numpy as jnp
from jax import lax
from jax.sharding import PartitionSpec as P

MODE = 256


def broadcast(block, axis, holder):
    block = jnp.where(lax.axis_index(axis) == holder, block, jnp.zeros_like(block))
    return lax.psum(block, axis)


def product(left_mat, right_mat):
    return jnp.dot(
        left_mat, right_mat, precision=lax.Precision.HIGHEST, preferred_element_type=jnp.float32
    )


def orthonormal(gram_matrix, sketch):
    powered = product(gram_matrix, product(gram_matrix, sketch))
    chol_low = jnp.linalg.cholesky(product(powered.T, powered))
    return jax.scipy.linalg.solve_triangular(chol_low, powered.T, lower=True).T


def local(train_cores, sketch, exit_sketch):
    block_core = train_cores[0]
    full_rank = block_core.shape[0]
    mode_count = block_core.shape[1]
    kept_rank = sketch.shape[1]
    chain_len = lax.axis_size("cores")
    position = lax.axis_index("cores")
    vector_count = lax.axis_size("vec")
    identity = jnp.eye(full_rank, dtype=jnp.float32)
    zero_square = jnp.zeros((full_rank, full_rank), jnp.float32)
    row_major = block_core.reshape(full_rank * mode_count, full_rank)
    wide_core = block_core.reshape(full_rank, mode_count * full_rank)

    def forward_gram(lower_in):
        absorbed = product(lower_in.T, wide_core).reshape(full_rank * mode_count, full_rank)
        return product(absorbed.T, absorbed)

    def zero_gram(operand):
        return zero_square

    lower_prev = identity
    lower_own = identity
    gram_own = identity
    for link_index in range(chain_len):
        active = position == link_index
        partial_value = lax.cond(active, forward_gram, zero_gram, lower_prev)
        summed = jnp.where(active, lax.psum(partial_value, "row"), identity)
        factor = jnp.linalg.cholesky(summed)
        if link_index + 1 < chain_len:
            arrived = broadcast(factor, "cores", link_index)
            lower_prev = jnp.where(position == link_index + 1, arrived, lower_prev)
        lower_own = jnp.where(active, factor, lower_own)
        gram_own = jnp.where(active, summed, gram_own)
    is_last = position == chain_len - 1
    incoming = orthonormal(gram_own, exit_sketch)

    def right_map_of(incoming_frame):
        solved = jax.scipy.linalg.solve_triangular(lower_own, incoming_frame, lower=True, trans=1)
        return jnp.where(is_last, incoming_frame, solved)

    def backward_gram(incoming_frame):
        reduced = product(row_major, right_map_of(incoming_frame)).reshape(
            full_rank, mode_count * kept_rank
        )
        mixed_core = product(lower_prev.T, reduced)
        return product(mixed_core, mixed_core.T)

    frame_own = jnp.zeros((full_rank, kept_rank), jnp.float32)
    for link_index in range(chain_len):
        target = chain_len - 1 - link_index
        active = position == target
        partial_value = lax.cond(active, backward_gram, zero_gram, incoming)
        summed = jnp.where(active, lax.psum(partial_value, "row"), identity)
        frame = orthonormal(summed, sketch)
        if target > 0:
            arrived = broadcast(frame, "cores", target)
            incoming = jnp.where(position == target - 1, arrived, incoming)
        frame_own = jnp.where(active, frame, frame_own)
    reduced = product(row_major, right_map_of(incoming)).reshape(full_rank, mode_count * kept_rank)
    front_map = product(frame_own.T, lower_prev.T)
    shaped = product(front_map, reduced)
    rounded = (shaped * math.sqrt(kept_rank * MODE)).reshape(1, kept_rank, mode_count, kept_rank)
    bases_out = (frame_own * math.sqrt(full_rank))[None]
    gathered, frames_all = (
        lax.all_gather(shaped[None], "vec", axis=0, tiled=True),
        lax.all_gather(frame_own[None], "vec", axis=0, tiled=True),
    )
    start_env = jnp.einsum("az,qay->qzy", frame_own, frames_all, precision=lax.Precision.HIGHEST)
    mine_rows = shaped.reshape(kept_rank * mode_count, kept_rank)
    zero_env = jnp.zeros((vector_count, kept_rank, kept_rank), jnp.float32)

    def margin_terms(env_in):
        carried = jnp.einsum("qzw,qwx->qzx", env_in, gathered, precision=lax.Precision.HIGHEST)
        carried = carried.reshape(vector_count, kept_rank * mode_count, kept_rank)
        return jnp.einsum("cb,qcy->qby", mine_rows, carried, precision=lax.Precision.HIGHEST)

    def zero_margin(operand):
        return zero_env

    env_in = start_env
    env_own = zero_env
    for link_index in range(chain_len):
        active = position == link_index
        partial_value = lax.cond(active, margin_terms, zero_margin, env_in)
        summed = lax.psum(partial_value, "row")
        if link_index + 1 < chain_len:
            arrived = broadcast(summed, "cores", link_index)
            env_in = jnp.where(position == link_index + 1, arrived, env_in)
        env_own = jnp.where(active, summed, env_own)
    margins = env_own.transpose(1, 0, 2).reshape(kept_rank, vector_count * kept_rank)[None]
    return (rounded, bases_out, margins)


def solution(mesh):
    return jax.shard_map(
        local,
        mesh=mesh,
        in_specs=(P("vec", "cores", "row", None), P("cores", None), P()),
        out_specs=(
            P("vec", "cores", "row", None),
            P("vec", "cores", None),
            P("vec", "cores", None),
        ),
        check_vma=False,
    )
```

profile of v0, /device:TPU:1, one launch (start us, length us, event | category | flops | bytes accessed | tf_op | source)
XLA Modules:
  0.0 1188.9 jit_solution(5875113720510303117)
XLA Ops:
  16.3 119.6 %all-reduce.11.cloned.1.call-done = f32[256,256]{0,1:T(8,128)} async-done(((f32[256,256]{0,1:T(8,128)}), f32[256,256]{0,1:T(8,128)}) %all-reduce.11.cloned.1.call-update) | async-done | bytes 262160 | tf_op jit(solution)/shard_map/psum | solution.py:53
  136.2 11.7 cholesky.187
  148.0 9.8 custom-call.23
  158.4 11.7 cholesky.204
  173.1 32.5 %all-reduce.13.cloned.1.call-done = f32[256,256]{0,1:T(8,128)} async-done(((f32[256,256]{0,1:T(8,128)}), f32[256,256]{0,1:T(8,128)}) %all-reduce.13.cloned.1.call-update) | async-done | bytes 262160 | tf_op jit(solution)/shard_map/psum | solution.py:12
  206.6 23.0 %conditional.7 = (f32[256,256]{1,0:T(8,128)S(1)}) conditional(s32[]{:T(128)} %convert_element_type.28, () %tuple.49, (f32[256,256]{0,1:T(8,128)S(1)}, f32[256,4096]{1,0:T(8,128)}) %tuple.170), branch_computations={%region_8.10_spmd, %region_9.11_spmd} | conditional | flops 6442450944 | bytes 21495816 | solution.py:52
  206.6 8.2 fusion.96
  219.6 9.9 fusion.97
  230.7 93.4 %all-reduce.15.cloned.1.call-done = f32[256,256]{0,1:T(8,128)} async-done(((f32[256,256]{0,1:T(8,128)}), f32[256,256]{0,1:T(8,128)}) %all-reduce.15.cloned.1.call-update) | async-done | bytes 262160 | tf_op jit(solution)/shard_map/psum | solution.py:53
  326.2 11.7 cholesky.221
  338.1 9.8 custom-call.24
  348.5 11.7 cholesky.238
  364.0 12.1 %cholesky.253 = f32[128,128]{1,0:T(8,128)S(1)} custom-call(f32[128,128]{1,0:T(8,128)S(1)} %fusion.69), custom_call_target="Cholesky" | custom-call | tf_op jit(solution)/shard_map/jit(cholesky)/cholesky | solution.py:23
  377.4 9.8 custom-call.25
  390.3 42.7 %conditional.8 = (f32[256,256]{1,0:T(8,128)S(1)}) conditional(s32[]{:T(128)} %convert_element_type.28, () %tuple.53, (pred[]{:T(512)}, f32[256,256]{0,1:T(8,128)S(1)}, f32[256,128]{0,1:T(8,128)S(1)}, f32[4096,256]{1,0:T(8,128)}, f32[256,256]{0,1:T(8,128)S(1)}) %tuple.167), branch_computations={%region_13.17_spmd, %region_14.19_spmd} | conditional | flops 4907548672 | bytes 23855310 | solution.py:78
  394.6 19.7 %custom-call.21 = f32[2,128,128]{1,2,0:T(8,128)S(1)} custom-call(f32[2,128,128]{2,1,0:T(8,128)S(1)} %get-tuple-element.113), custom_call_target="InvertDiagBlocksLowerTriangular" | custom-call | tf_op jit(solution)/shard_map/cond/branch_1_fun/jit(_solve_triangular)/triangular_solve | solution.py:64
  433.9 91.5 %all-reduce.17.cloned.1.call-done = f32[256,256]{0,1:T(8,128)} async-done(((f32[256,256]{0,1:T(8,128)}), f32[256,256]{0,1:T(8,128)}) %all-reduce.17.cloned.1.call-update) | async-done | bytes 262160 | tf_op jit(solution)/shard_map/psum | solution.py:79
  529.0 11.7 cholesky.264
  542.1 9.8 custom-call.26
  552.9 28.4 %all-reduce.19.cloned.1.call-done = f32[256,128]{0,1:T(8,128)} async-done(((f32[256,128]{0,1:T(8,128)}), f32[256,128]{0,1:T(8,128)}) %all-reduce.19.cloned.1.call-update) | async-done | bytes 131088 | tf_op jit(solution)/shard_map/psum | solution.py:12
  588.6 131.1 %all-reduce.21.cloned.1.call-done = f32[256,256]{0,1:T(8,128)} async-done(((f32[256,256]{0,1:T(8,128)}), f32[256,256]{0,1:T(8,128)}) %all-reduce.21.cloned.1.call-update) | async-done | bytes 262160 | tf_op jit(solution)/shard_map/psum | solution.py:79
  721.5 11.7 cholesky.275
  734.5 9.8 custom-call.27
  749.7 19.7 %custom-call.28 = f32[2,128,128]{1,2,0:T(8,128)S(1)} custom-call(f32[2,128,128]{2,1,0:T(8,128)S(1)} %get-tuple-element.115), custom_call_target="InvertDiagBlocksLowerTriangular" | custom-call | tf_op jit(solution)/shard_map/jit(_solve_triangular)/triangular_solve | solution.py:64
  786.7 95.5 %all-gather.7.cloned.1.call-done = f32[1024,2048]{1,0:T(8,128)} async-done(((f32[128,2048]{1,0:T(8,128)}), f32[1024,2048]{1,0:T(8,128)}) %all-gather.7.cloned.1.call-update) | async-done | bytes 8388624 | tf_op jit(solution)/shard_map/all_gather | solution.py:91
  883.5 129.1 %all-reduce.23.cloned.1.call-done = f32[8,128,128]{1,2,0:T(8,128)} async-done(((f32[8,128,128]{1,2,0:T(8,128)}), f32[8,128,128]{1,2,0:T(8,128)}) %all-reduce.23.cloned.1.call-update) | async-done | bytes 524304 | tf_op jit(solution)/shard_map/psum | solution.py:111
  1013.5 33.1 %all-reduce.25.cloned.1.call-done = f32[8,128,128]{1,2,0:T(8,128)} async-done(((f32[8,128,128]{1,2,0:T(8,128)}), f32[8,128,128]{1,2,0:T(8,128)}) %all-reduce.25.cloned.1.call-update) | async-done | bytes 524304 | tf_op jit(solution)/shard_map/psum | solution.py:12
  1046.6 38.8 %conditional.11 = (f32[8,128,128]{1,2,0:T(8,128)}) conditional(s32[]{:T(128)} %convert_element_type.28, () %tuple.56, (pred[]{:T(512)}, f32[8,128,128]{1,2,0:T(8,128)}, f32[8,128,128]{1,2,0:T(8,128)S(1)}, f32[8,128,2048]{2,1,0:T(8,128)}, f32[2048,128]{1,0:T(8,128)S(1)}) %tuple.172), branch_computations={%region_24.29_spmd, %region_25.30_spmd} | conditional | flops 6442582016 | bytes 46661640 | solution.py:110
  1048.2 11.7 fusion.2
  1059.9 9.3 reshape.52
  1069.2 16.2 %convolution_bitcast_fusion.1 = f32[8,128,128]{1,2,0:T(8,128)} fusion(f32[8,2048,128]{2,1,0:T(8,128)} %reshape.52, f32[2048,128]{1,0:T(8,128)S(1)} %get-tuple-element.89), kind=kOutput, calls=%fused_computation.2 | convolution fusion | flops 3221225472 | bytes 9961472 | tf_op jit(solution)/shard_map/cond/branch_1_fun/cb,qcy->qby/dot_general | solution.py:101
  1087.4 92.6 %all-reduce.27.cloned.1.call-done = f32[8,128,128]{1,2,0:T(8,128)} async-done(((f32[8,128,128]{1,2,0:T(8,128)}), f32[8,128,128]{1,2,0:T(8,128)}) %all-reduce.27.cloned.1.call-update) | async-done | bytes 524304 | tf_op jit(solution)/shard_map/psum | solution.py:111
  (171 shorter events, 105.8 us)
Async XLA Ops:
  7.2 518.2 %copy-start = (f32[256,128]{1,0:T(8,128)S(1)}, f32[256,128]{1,0:T(8,128)}, u32[]{:S(2)}) copy-start(f32[256,128]{1,0:T(8,128)} %param.22) | copy-start | bytes 393220
  7.2 128.7 %all-reduce.11.cloned.1.call-start = ((), (), s32[]{:S(2)}) async-start(), calls=%async_computation | async-start | bytes 524288 | tf_op jit(solution)/shard_map/psum | solution.py:53
  16.1 189.5 %all-reduce.13.cloned.1.call-start = ((), (), s32[]{:S(2)}) async-start(), calls=%async_computation.1 | async-start | bytes 524288 | tf_op jit(solution)/shard_map/psum | solution.py:12
  173.0 151.1 %all-reduce.15.cloned.1.call-start = ((), (), s32[]{:S(2)}) async-start(), calls=%async_computation.2 | async-start | bytes 524288 | tf_op jit(solution)/shard_map/psum | solution.py:53
  206.5 153.8 %copy-start.3 = (f32[256,256]{0,1:T(8,128)S(1)}, f32[256,256]{0,1:T(8,128)}, u32[]{:S(2)}) copy-start(f32[256,256]{0,1:T(8,128)} %all-reduce.11.cloned.1.call-done) | copy-start | bytes 786436
  206.6 153.8 %copy-start.8 = (f32[256,128]{1,0:T(8,128)S(1)}, f32[256,128]{1,0:T(8,128)}, u32[]{:S(2)}) copy-start(f32[256,128]{1,0:T(8,128)} %param.23) | copy-start | bytes 393220
  230.4 295.0 %all-reduce.17.cloned.1.call-start = ((), (), s32[]{:S(2)}) async-start(), calls=%async_computation.3 | async-start | bytes 524288 | tf_op jit(solution)/shard_map/psum | solution.py:79
  433.8 147.4 %all-reduce.19.cloned.1.call-start = ((), (), s32[]{:S(2)}) async-start(), calls=%async_computation.4 | async-start | bytes 262144 | tf_op jit(solution)/shard_map/psum | solution.py:12
  552.9 166.9 %all-reduce.21.cloned.1.call-start = ((), (), s32[]{:S(2)}) async-start(), calls=%async_computation.5 | async-start | bytes 524288 | tf_op jit(solution)/shard_map/psum | solution.py:79
  581.3 163.0 %copy-start.7 = (f32[256,128]{0,1:T(8,128)S(1)}, f32[256,128]{0,1:T(8,128)}, u32[]{:S(2)}) copy-start(f32[256,128]{0,1:T(8,128)} %fusion.24) | copy-start | bytes 393220
  588.6 195.9 %all-gather.5.cloned.1.call-start = ((), (), s32[]{:S(2)}) async-start(), calls=%async_computation.9 | async-start | bytes 1179648 | tf_op jit(solution)/shard_map/all_gather | solution.py:92
  745.3 136.8 %all-gather.7.cloned.1.call-start = ((), (), s32[]{:S(2)}) async-start(), calls=%async_computation.10 | async-start | bytes 9437184 | tf_op jit(solution)/shard_map/all_gather | solution.py:91
  776.8 3.6 copy-start.4
  783.0 229.6 %all-reduce.23.cloned.1.call-start = ((), (), s32[]{:S(2)}) async-start(), calls=%async_computation.6 | async-start | bytes 1048576 | tf_op jit(solution)/shard_map/psum | solution.py:111
  882.6 0.8 copy-start.5
  883.4 163.2 %all-reduce.25.cloned.1.call-start = ((), (), s32[]{:S(2)}) async-start(), calls=%async_computation.7 | async-start | bytes 1048576 | tf_op jit(solution)/shard_map/psum | solution.py:12
  1013.4 166.6 %all-reduce.27.cloned.1.call-start = ((), (), s32[]{:S(2)}) async-start(), calls=%async_computation.8 | async-start | bytes 1048576 | tf_op jit(solution)/shard_map/psum | solution.py:111
  1046.6 39.6 %copy-start.2 = (f32[128,2048]{1,0:T(8,128)S(1)}, f32[128,2048]{1,0:T(8,128)}, u32[]{:S(2)}) copy-start(f32[128,2048]{1,0:T(8,128)} %fusion.107) | copy-start | bytes 3145732
  1085.4 94.7 %copy-start.6 = (f32[8,128,128]{1,2,0:T(8,128)S(1)}, f32[8,128,128]{1,2,0:T(8,128)}, u32[]{:S(2)}) copy-start(f32[8,128,128]{1,2,0:T(8,128)} %all-reduce.23.cloned.1.call-done) | copy-start | bytes 1572868
  1085.4 96.8 %copy-start.1 = (f32[256,128]{1,0:T(8,128)S(1)}, f32[256,128]{1,0:T(8,128)}, u32[]{:S(2)}) copy-start(f32[256,128]{1,0:T(8,128)} %param.22) | copy-start | bytes 393220
Sparse Core Ops, SparseCore 0:
  16.2 119.6 all-reduce.10
  173.2 32.3 all-reduce.12
  230.5 93.5 all-reduce.14
  434.0 91.3 all-reduce.16
  553.0 28.2 all-reduce.18
  588.7 131.0 all-reduce.20
  745.5 37.0 all-gather.4
  785.1 96.9 all-gather.6
  886.2 126.2 all-reduce.22
  1015.6 30.9 all-reduce.24
  1085.5 94.4 all-reduce.26
where the time goes:
time: 1200 us; the launch traced here: 1190 us
  waiting for transfers between devices  847 us (71%)
  other arithmetic  183 us (15%)
  matrix products  84.3 us (7%)
  local copies, waits for them, and re-layouts  48.8 us (4%)
  between operations  17.2 us (1%)
    psum x4, waiting for transfers between devices, local(): summed = jnp.where(active, lax.psum(partial_value, 'row'), identity)  436 us
    psum x2, waiting for transfers between devices, local(): summed = lax.psum(partial_value, 'row')  222 us
    all_gather x1, waiting for transfers between devices, local(): lax.all_gather(shaped[None], 'vec', axis=0, tiled=True)  95.5 us
    psum x3, waiting for transfers between devices, broadcast(): return lax.psum(block, axis)  94 us
    another operation x13, other arithmetic, local(): factor = jnp.linalg.cholesky(summed)  68.5 us
    dot_general x17, matrix products, product(): jnp.dot(left_mat, right_mat, precision=lax.Precision.HIGHEST, preferred_e...  49.5 us
    another operation x8, other arithmetic, right_map_of(): jax.scipy.linalg.solve_triangular(lower_own, incoming_frame, lower=True,...  39.4 us
    another operation x9, other arithmetic, orthonormal(): chol_low = jnp.linalg.cholesky(product(powered.T, powered))  37.6 us
  transfers between devices with their start and end apart: 11, of which 10 were waited for; matrix products, arithmetic and copies ran while one was open for 4% of the time, Pallas kernels for 0%

commit v1 on v0

--- a/solution.py
+++ b/solution.py
@@ -76,7 +76,7 @@
         target = chain_len - 1 - link_index
         active = position == target
         partial_value = lax.cond(active, backward_gram, zero_gram, incoming)
-        summed = jnp.where(active, lax.psum(partial_value, "row"), identity)
+        summed = jnp.where(active, jnp.sum(lax.all_gather(partial_value, "row"), axis=0), identity)
         frame = orthonormal(summed, sketch)
         if target > 0:
             arrived = broadcast(frame, "cores", target)

time: 1200 us -> 1130 us (0.942)
  waiting for transfers between devices: 847 us -> 772 us
    psum x4 -> x2, waiting for transfers between devices: 436 us -> 213 us  [local(): summed = jnp.where(active, lax.psum(partial_value, 'row'), identity)]
    all_gather x0 -> x2, waiting for transfers between devices: none -> 149 us  [local(): lax.all_gather(partial_value, 'row')]
where the time goes in v1:
time: 1130 us; the launch traced here: 1120 us
  waiting for transfers between devices  772 us (68%)
  other arithmetic  188 us (17%)
  matrix products  82.3 us (7%)
  local copies, waits for them, and re-layouts  48.8 us (4%)
  between operations  17.3 us (2%)
    psum x2, waiting for transfers between devices, local(): summed = lax.psum(partial_value, 'row')  222 us
    psum x2, waiting for transfers between devices, local(): summed = jnp.where(active, lax.psum(partial_value, 'row'), identity)  213 us
    all_gather x2, waiting for transfers between devices, local(): lax.all_gather(partial_value, 'row')  149 us
    psum x3, waiting for transfers between devices, broadcast(): return lax.psum(block, axis)  94.9 us
    all_gather x1, waiting for transfers between devices, local(): lax.all_gather(shaped[None], 'vec', axis=0, tiled=True)  92.4 us
    another operation x13, other arithmetic, local(): factor = jnp.linalg.cholesky(summed)  68.5 us
    dot_general x17, matrix products, product(): jnp.dot(left_mat, right_mat, precision=lax.Precision.HIGHEST, preferred_e...  47.5 us
    another operation x8, other arithmetic, right_map_of(): jax.scipy.linalg.solve_triangular(lower_own, incoming_frame, lower=True,...  39.4 us
  transfers between devices with their start and end apart: 11, of which 10 were waited for; matrix products, arithmetic and copies ran while one was open for 4% of the time, Pallas kernels for 0%

profile of v1, /device:TPU:1, one launch (start us, length us, event | category | flops | bytes accessed | tf_op | source)
XLA Modules:
  0.0 1116.8 jit_solution(9902548976594552276)
XLA Ops:
  16.3 119.6 %all-reduce.9.cloned.1.call-done = f32[256,256]{0,1:T(8,128)} async-done(((f32[256,256]{0,1:T(8,128)}), f32[256,256]{0,1:T(8,128)}) %all-reduce.9.cloned.1.call-update) | async-done | bytes 262160 | tf_op jit(solution)/shard_map/psum | solution.py:53
  136.2 11.7 %cholesky.187 = f32[128,128]{1,0:T(8,128)S(1)} custom-call(f32[128,128]{1,0:T(8,128)S(1)} %cholesky.284), custom_call_target="Cholesky" | custom-call | tf_op jit(solution)/shard_map/jit(cholesky)/cholesky | solution.py:54
  148.0 9.8 custom-call.23
  158.4 11.7 %cholesky.204 = f32[128,128]{1,0:T(8,128)S(1)} custom-call(f32[128,128]{1,0:T(8,128)S(1)} %convolution_subtract_fusion.4), custom_call_target="Cholesky" | custom-call | tf_op jit(solution)/shard_map/jit(cholesky)/cholesky | solution.py:54
  173.1 32.5 %all-reduce.11.cloned.1.call-done = f32[256,256]{0,1:T(8,128)} async-done(((f32[256,256]{0,1:T(8,128)}), f32[256,256]{0,1:T(8,128)}) %all-reduce.11.cloned.1.call-update) | async-done | bytes 262160 | tf_op jit(solution)/shard_map/psum | solution.py:12
  206.6 23.0 %conditional.7 = (f32[256,256]{1,0:T(8,128)S(1)}) conditional(s32[]{:T(128)} %convert_element_type.28, () %tuple.49, (f32[256,256]{0,1:T(8,128)S(1)}, f32[256,4096]{1,0:T(8,128)}) %tuple.178), branch_computations={%region_8.10_spmd, %region_9.11_spmd} | conditional | flops 6442450944 | bytes 21495816 | solution.py:52
  206.6 8.2 fusion.96
  219.6 9.9 fusion.97
  230.7 93.4 %all-reduce.13.cloned.1.call-done = f32[256,256]{0,1:T(8,128)} async-done(((f32[256,256]{0,1:T(8,128)}), f32[256,256]{0,1:T(8,128)}) %all-reduce.13.cloned.1.call-update) | async-done | bytes 262160 | tf_op jit(solution)/shard_map/psum | solution.py:53
  326.2 11.7 %cholesky.221 = f32[128,128]{1,0:T(8,128)S(1)} custom-call(f32[128,128]{1,0:T(8,128)S(1)} %cholesky.287), custom_call_target="Cholesky" | custom-call | tf_op jit(solution)/shard_map/jit(cholesky)/cholesky | solution.py:54
  338.1 9.8 custom-call.24
  348.5 11.7 %cholesky.238 = f32[128,128]{1,0:T(8,128)S(1)} custom-call(f32[128,128]{1,0:T(8,128)S(1)} %convolution_subtract_fusion.3), custom_call_target="Cholesky" | custom-call | tf_op jit(solution)/shard_map/jit(cholesky)/cholesky | solution.py:54
  364.0 12.1 %cholesky.253 = f32[128,128]{1,0:T(8,128)S(1)} custom-call(f32[128,128]{1,0:T(8,128)S(1)} %fusion.69), custom_call_target="Cholesky" | custom-call | tf_op jit(solution)/shard_map/jit(cholesky)/cholesky | solution.py:23
  377.4 9.8 custom-call.25
  390.3 42.7 %conditional.8 = (f32[256,256]{1,0:T(8,128)S(1)}) conditional(s32[]{:T(128)} %convert_element_type.28, () %tuple.53, (pred[]{:T(512)}, f32[256,256]{0,1:T(8,128)S(1)}, f32[256,128]{0,1:T(8,128)S(1)}, f32[4096,256]{1,0:T(8,128)}, f32[256,256]{0,1:T(8,128)S(1)}) %tuple.175), branch_computations={%region_13.17_spmd, %region_14.19_spmd} | conditional | flops 4907548672 | bytes 23855310 | solution.py:78
  394.6 19.7 %custom-call.21 = f32[2,128,128]{1,2,0:T(8,128)S(1)} custom-call(f32[2,128,128]{2,1,0:T(8,128)S(1)} %get-tuple-element.113), custom_call_target="InvertDiagBlocksLowerTriangular" | custom-call | tf_op jit(solution)/shard_map/cond/branch_1_fun/jit(_solve_triangular)/triangular_solve | solution.py:64
  433.8 55.0 %all-gather.9.cloned.1.call-done = f32[4096,256]{1,0:T(8,128)} async-done(((f32[256,256]{1,0:T(8,128)}), f32[4096,256]{1,0:T(8,128)}) %all-gather.9.cloned.1.call-update) | async-done | bytes 4194320 | tf_op jit(solution)/shard_map/all_gather | solution.py:79
  493.1 11.7 %cholesky.264 = f32[128,128]{1,0:T(8,128)S(1)} custom-call(f32[128,128]{1,0:T(8,128)S(1)} %fusion.67), custom_call_target="Cholesky" | custom-call | tf_op jit(solution)/shard_map/jit(cholesky)/cholesky | solution.py:23
  506.2 9.8 custom-call.26
  517.0 29.3 %all-reduce.15.cloned.1.call-done = f32[256,128]{0,1:T(8,128)} async-done(((f32[256,128]{0,1:T(8,128)}), f32[256,128]{0,1:T(8,128)}) %all-reduce.15.cloned.1.call-update) | async-done | bytes 131088 | tf_op jit(solution)/shard_map/psum | solution.py:12
  553.7 94.5 %all-gather.11.cloned.1.call-done = f32[4096,256]{1,0:T(8,128)} async-done(((f32[256,256]{1,0:T(8,128)}), f32[4096,256]{1,0:T(8,128)}) %all-gather.11.cloned.1.call-update) | async-done | bytes 4194320 | tf_op jit(solution)/shard_map/all_gather | solution.py:79
  652.5 11.7 %cholesky.275 = f32[128,128]{1,0:T(8,128)S(1)} custom-call(f32[128,128]{1,0:T(8,128)S(1)} %fusion.65), custom_call_target="Cholesky" | custom-call | tf_op jit(solution)/shard_map/jit(cholesky)/cholesky | solution.py:23
  665.5 9.8 custom-call.27
  680.7 19.7 %custom-call.28 = f32[2,128,128]{1,2,0:T(8,128)S(1)} custom-call(f32[2,128,128]{2,1,0:T(8,128)S(1)} %get-tuple-element.115), custom_call_target="InvertDiagBlocksLowerTriangular" | custom-call | tf_op jit(solution)/shard_map/jit(_solve_triangular)/triangular_solve | solution.py:64
  717.7 92.4 %all-gather.15.cloned.1.call-done = f32[1024,2048]{1,0:T(8,128)} async-done(((f32[128,2048]{1,0:T(8,128)}), f32[1024,2048]{1,0:T(8,128)}) %all-gather.15.cloned.1.call-update) | async-done | bytes 8388624 | tf_op jit(solution)/shard_map/all_gather | solution.py:91
  811.4 129.1 %all-reduce.17.cloned.1.call-done = f32[8,128,128]{1,2,0:T(8,128)} async-done(((f32[8,128,128]{1,2,0:T(8,128)}), f32[8,128,128]{1,2,0:T(8,128)}) %all-reduce.17.cloned.1.call-update) | async-done | bytes 524304 | tf_op jit(solution)/shard_map/psum | solution.py:111
  941.4 33.1 %all-reduce.19.cloned.1.call-done = f32[8,128,128]{1,2,0:T(8,128)} async-done(((f32[8,128,128]{1,2,0:T(8,128)}), f32[8,128,128]{1,2,0:T(8,128)}) %all-reduce.19.cloned.1.call-update) | async-done | bytes 524304 | tf_op jit(solution)/shard_map/psum | solution.py:12
  974.5 38.8 %conditional.11 = (f32[8,128,128]{1,2,0:T(8,128)}) conditional(s32[]{:T(128)} %convert_element_type.28, () %tuple.56, (pred[]{:T(512)}, f32[8,128,128]{1,2,0:T(8,128)}, f32[8,128,128]{1,2,0:T(8,128)S(1)}, f32[8,128,2048]{2,1,0:T(8,128)}, f32[2048,128]{1,0:T(8,128)S(1)}) %tuple.180), branch_computations={%region_24.29_spmd, %region_25.30_spmd} | conditional | flops 6442582016 | bytes 46661640 | solution.py:110
  976.1 11.7 %fusion.2 = f32[8,128,2048]{2,1,0:T(8,128)} fusion(f32[8,128,2048]{2,1,0:T(8,128)} %get-tuple-element.88, f32[8,128,128]{2,1,0:T(8,128)S(1)} %copy.108, f32[8,128,128]{2,1,0:T(8,128)S(1)} %copy.109, pred[]{:T(512)} %get-tuple-element.85), kind=kOutput, calls=%fused_computation.4 | convolution fusion | flops 3221356544 | bytes 17825792 | tf_op jit(solution)/shard_map/cond/branch_1_fun/qzw,qwx->qzx/dot_general | solution.py:99
  987.8 9.3 reshape.52
  997.1 16.2 %convolution_bitcast_fusion.1 = f32[8,128,128]{1,2,0:T(8,128)} fusion(f32[8,2048,128]{2,1,0:T(8,128)} %reshape.52, f32[2048,128]{1,0:T(8,128)S(1)} %get-tuple-element.89), kind=kOutput, calls=%fused_computation.2 | convolution fusion | flops 3221225472 | bytes 9961472 | tf_op jit(solution)/shard_map/cond/branch_1_fun/cb,qcy->qby/dot_general | solution.py:101
  1015.4 92.6 %all-reduce.21.cloned.1.call-done = f32[8,128,128]{1,2,0:T(8,128)} async-done(((f32[8,128,128]{1,2,0:T(8,128)}), f32[8,128,128]{1,2,0:T(8,128)}) %all-reduce.21.cloned.1.call-update) | async-done | bytes 524304 | tf_op jit(solution)/shard_map/psum | solution.py:111
  (177 shorter events, 109.0 us)
Async XLA Ops:
  7.2 484.2 %copy-start = (f32[256,128]{1,0:T(8,128)S(1)}, f32[256,128]{1,0:T(8,128)}, u32[]{:S(2)}) copy-start(f32[256,128]{1,0:T(8,128)} %param.22) | copy-start | bytes 393220
  7.2 128.7 %all-reduce.9.cloned.1.call-start = ((), (), s32[]{:S(2)}) async-start(), calls=%async_computation | async-start | bytes 524288 | tf_op jit(solution)/shard_map/psum | solution.py:53
  16.1 189.5 %all-reduce.11.cloned.1.call-start = ((), (), s32[]{:S(2)}) async-start(), calls=%async_computation.1 | async-start | bytes 524288 | tf_op jit(solution)/shard_map/psum | solution.py:12
  173.0 151.1 %all-reduce.13.cloned.1.call-start = ((), (), s32[]{:S(2)}) async-start(), calls=%async_computation.2 | async-start | bytes 524288 | tf_op jit(solution)/shard_map/psum | solution.py:53
  206.5 153.8 %copy-start.3 = (f32[256,256]{0,1:T(8,128)S(1)}, f32[256,256]{0,1:T(8,128)}, u32[]{:S(2)}) copy-start(f32[256,256]{0,1:T(8,128)} %all-reduce.9.cloned.1.call-done) | copy-start | bytes 786436
  206.6 153.8 %copy-start.10 = (f32[256,128]{1,0:T(8,128)S(1)}, f32[256,128]{1,0:T(8,128)}, u32[]{:S(2)}) copy-start(f32[256,128]{1,0:T(8,128)} %param.23) | copy-start | bytes 393220
  230.4 258.4 %all-gather.9.cloned.1.call-start = ((), (), s32[]{:S(2)}) async-start(), calls=%async_computation.7 | async-start | bytes 4456448 | tf_op jit(solution)/shard_map/all_gather | solution.py:79
  433.0 0.7 copy-start.8
  433.7 112.6 %all-reduce.15.cloned.1.call-start = ((), (), s32[]{:S(2)}) async-start(), calls=%async_computation.3 | async-start | bytes 262144 | tf_op jit(solution)/shard_map/psum | solution.py:12
  517.0 131.2 %all-gather.11.cloned.1.call-start = ((), (), s32[]{:S(2)}) async-start(), calls=%async_computation.8 | async-start | bytes 4456448 | tf_op jit(solution)/shard_map/all_gather | solution.py:79
  552.9 0.7 copy-start.9
  552.9 122.4 %copy-start.7 = (f32[256,128]{0,1:T(8,128)S(1)}, f32[256,128]{0,1:T(8,128)}, u32[]{:S(2)}) copy-start(f32[256,128]{0,1:T(8,128)} %fusion.24) | copy-start | bytes 393220
  553.6 161.8 %all-gather.13.cloned.1.call-start = ((), (), s32[]{:S(2)}) async-start(), calls=%async_computation.9 | async-start | bytes 1179648 | tf_op jit(solution)/shard_map/all_gather | solution.py:92
  676.4 133.7 %all-gather.15.cloned.1.call-start = ((), (), s32[]{:S(2)}) async-start(), calls=%async_computation.10 | async-start | bytes 9437184 | tf_op jit(solution)/shard_map/all_gather | solution.py:91
  707.8 3.6 copy-start.4
  714.0 226.5 %all-reduce.17.cloned.1.call-start = ((), (), s32[]{:S(2)}) async-start(), calls=%async_computation.4 | async-start | bytes 1048576 | tf_op jit(solution)/shard_map/psum | solution.py:111
  810.5 0.8 copy-start.5
  811.3 163.2 %all-reduce.19.cloned.1.call-start = ((), (), s32[]{:S(2)}) async-start(), calls=%async_computation.5 | async-start | bytes 1048576 | tf_op jit(solution)/shard_map/psum | solution.py:12
  941.4 166.6 %all-reduce.21.cloned.1.call-start = ((), (), s32[]{:S(2)}) async-start(), calls=%async_computation.6 | async-start | bytes 1048576 | tf_op jit(solution)/shard_map/psum | solution.py:111
  974.5 39.6 %copy-start.2 = (f32[128,2048]{1,0:T(8,128)S(1)}, f32[128,2048]{1,0:T(8,128)}, u32[]{:S(2)}) copy-start(f32[128,2048]{1,0:T(8,128)} %fusion.107) | copy-start | bytes 3145732
  1013.3 94.7 %copy-start.6 = (f32[8,128,128]{1,2,0:T(8,128)S(1)}, f32[8,128,128]{1,2,0:T(8,128)}, u32[]{:S(2)}) copy-start(f32[8,128,128]{1,2,0:T(8,128)} %all-reduce.17.cloned.1.call-done) | copy-start | bytes 1572868
  1013.3 96.8 %copy-start.1 = (f32[256,128]{1,0:T(8,128)S(1)}, f32[256,128]{1,0:T(8,128)}, u32[]{:S(2)}) copy-start(f32[256,128]{1,0:T(8,128)} %param.22) | copy-start | bytes 393220
Sparse Core Ops, SparseCore 0:
  16.2 119.6 all-reduce.8
  173.2 32.3 all-reduce.10
  230.5 93.5 all-reduce.12
  433.8 54.9 all-gather.8
  517.1 29.1 all-reduce.14
  553.8 94.3 all-gather.10
  676.5 34.2 all-gather.12
  714.1 95.9 all-gather.14
  814.2 126.2 all-reduce.16
  943.5 30.9 all-reduce.18
  1013.5 94.4 all-reduce.20
